TPU v7x, 32 devices: a whole 2x2x4 slice. The times are simulated.
32 devices in a mesh: grp: 2 (over x), cell: 16 (over z, y, core).
Axes of the slice: x: 2, y: 2, z: 4, core: 2. Of those that a mesh axis runs over, the one named last changes fastest.
Arguments:
- fields: bfloat16 [8192, 3, 8192], P(('grp', 'cell')), parts along dimension 0, may hold values from -6 to 6
- horiz: float32 [16384], P(('grp', 'cell')), parts along dimension 0, may hold values from 0.2 to 1
- vertical: float32 [16384], P(('grp', 'cell')), parts along dimension 0, may hold values from 1.5 to 6
- tilt_angle: float32 [16384], P(('grp', 'cell')), parts along dimension 0, may hold values from 0.2 to 1.4
- azimuth: float32 [16384], P(('grp', 'cell')), parts along dimension 0, may hold values from -3.140625 to 3.140625
- electrode_quads: int32 [4096, 4], P('grp'), parts along dimension 0, may hold values from 0 to 4095, as said below
Outputs:
- jacobian: bfloat16 [4096, 4, 8192], P('grp', None, 'cell'), parts along dimension 0
- coverage: float32 [16384], P(('grp', 'cell')), parts along dimension 0
There are 2 independent parts, one for each index of `grp`. A program takes and returns all parts, laid end to end along the dimension named above; each array names one. Nothing has to cross between parts.
Inputs may be any that keep to these rules, and one draw needn't show every extreme that they name: `electrode_quads`: each row names four different electrodes.
All inputs are finite; a program needn't handle non-finite values.
Results may differ from a plain program's by a relative error of at most 0.001.
Values may be sent and summed in bfloat16 or wider, within the bound.
A program may use at most 192 MiB of HBM per device.

v0:
```python
import jax
import jax.numpy as jnp
from jax import lax
from jax.sharding import PartitionSpec as P


def sensitivity(grads, horiz, vertical, tilt_angle, azimuth, rows):

    def pick(column):
        return jnp.take(grads, rows[:, column], axis=0).astype(jnp.float32)

    source = pick(0) - pick(1)
    receiver = pick(2) - pick(3)
    sin_t = jnp.sin(tilt_angle)
    cos_t = jnp.cos(tilt_angle)
    sin_p = jnp.sin(azimuth)
    cos_p = jnp.cos(azimuth)
    axis_dir = jnp.stack([sin_t * cos_p, sin_t * sin_p, cos_t])
    tilt_dir = jnp.stack([cos_t * cos_p, cos_t * sin_p, -sin_t])
    turn_dir = jnp.stack([-sin_t * sin_p, sin_t * cos_p, jnp.zeros_like(sin_t)])

    def along(field, direction):
        return jnp.sum(field * direction[None], axis=1)

    s_axis = along(source, axis_dir)
    r_axis = along(receiver, axis_dir)
    s_tilt = along(source, tilt_dir)
    r_tilt = along(receiver, tilt_dir)
    s_turn = along(source, turn_dir)
    r_turn = along(receiver, turn_dir)
    inner = jnp.sum(source * receiver, axis=1)
    contrast = vertical - horiz
    return jnp.stack(
        [
            -horiz * (inner - s_axis * r_axis),
            -vertical * s_axis * r_axis,
            -contrast * (s_tilt * r_axis + s_axis * r_tilt),
            -contrast * (s_turn * r_axis + s_axis * r_turn),
        ],
        axis=1,
    )


def local(fields, horiz, vertical, tilt_angle, azimuth, electrode_quads):
    shards = lax.axis_size("cell")
    cell_dev = horiz.shape[0]
    local_fields = lax.all_to_all(fields, "cell", split_axis=2, concat_axis=0, tiled=True)
    values = sensitivity(local_fields, horiz, vertical, tilt_angle, azimuth, electrode_quads)
    partial_sq = jnp.sum(values * values, axis=(1, 2))
    total_sq = lax.psum(partial_sq, "cell")
    meansq = total_sq / (4.0 * cell_dev * shards)
    normed = values * lax.rsqrt(meansq + 1e-06)[:, None, None]
    return (normed.astype(jnp.bfloat16), jnp.sum(normed * normed, axis=(0, 1)))


def solution(mesh):
    placed = (
        P(("grp", "cell"), None, None),
        P(("grp", "cell")),
        P(("grp", "cell")),
        P(("grp", "cell")),
        P(("grp", "cell")),
        P("grp", None),
    )
    return jax.shard_map(
        local,
        mesh=mesh,
        in_specs=placed,
        out_specs=(P("grp", None, "cell"), P(("grp", "cell"))),
        check_vma=False,
    )
```

profile of v0, /device:TPU:0, one launch (start us, length us, event | category | flops | bytes accessed | tf_op | source)
XLA Modules:
  0.0 745.1 jit_solution(583494292606352755)
XLA Ops:
  0.6 25.0 %copy.16 = bf16[256,3,8192]{0,1,2:T(4,128)(2,1)} copy(bf16[256,3,8192]{2,0,1:T(8,128)(2,1)} %param.8) | data formatting | bytes 25165824 | tf_op args[0]
  25.6 0.0 copy-start.5
  25.6 0.0 copy-start.6
  25.6 0.0 copy-start.3
  25.6 0.0 copy-start.4
  25.6 0.0 copy-start.2
  25.6 7.6 %all-to-all-start = ((bf16[256,3,8192]{0,1,2:T(4,128)(2,1)}), bf16[256,3,8192]{0,1,2:T(4,128)(2,1)}, u32[]{:S(2)}, u32[]{:S(2)}) async-start(bf16[256,3,8192]{0,1,2:T(4,128)(2,1)} %copy.16), calls=%async_computation | async-start | bytes 33554432 | tf_op jit(solution)/shard_map/all_to_all | solution.py:47
  33.2 0.1 pad.6.clone
  33.3 0.0 copy-done.5
  33.3 0.0 copy-done.6
  33.4 0.0 copy-done.3
  33.4 0.0 copy-done.4
  33.4 0.0 copy-done.2
  33.5 0.1 pad_maximum_fusion.1
  33.6 296.4 %all-to-all-done = bf16[256,3,8192]{0,1,2:T(4,128)(2,1)} async-done(((bf16[256,3,8192]{0,1,2:T(4,128)(2,1)}), bf16[256,3,8192]{0,1,2:T(4,128)(2,1)}, u32[]{:S(2)}, u32[]{:S(2)}) %all-to-all-start) | async-done | bytes 12582944 | tf_op jit(solution)/shard_map/all_to_all | solution.py:47
  330.0 13.2 %copy.17 = bf16[256,3,8192]{0,2,1:T(8,128)(2,1)} copy(bf16[256,3,8192]{0,1,2:T(4,128)(2,1)} %all-to-all-done) | data formatting | bytes 25165824 | tf_op jit(solution)/shard_map/all_to_all | solution.py:47
  343.1 16.6 %copy.18 = bf16[16,256,3,512]{3,1,0,2:T(8,128)(2,1)} copy(bf16[16,256,3,512]{1,3,0,2:T(8,128)(2,1)} %bitcast.54) | data formatting | bytes 25165824 | tf_op jit(solution)/shard_map/all_to_all | solution.py:47
  359.7 18.9 %copy.19 = bf16[4096,3,512]{2,1,0:T(4,128)(2,1)} copy(bf16[4096,3,512]{2,0,1:T(8,128)(2,1)} %bitcast.55) | data formatting | bytes 25165824 | tf_op jit(solution)/shard_map/all_to_all | solution.py:47
  378.6 26.7 %gather_fusion = bf16[2048,3,512]{2,1,0:T(4,128)(2,1)} fusion(bf16[4096,3,512]{2,1,0:T(4,128)(2,1)} %copy.19, s32[2048]{0:T(1024)S(1)} %fusion.6), kind=kCustom, calls=%fused_computation.clone | custom fusion | bytes 12591104 | tf_op jit(solution)/shard_map/jit(_take)/gather | solution.py:10
  405.2 26.9 %gather_fusion.1 = bf16[2048,3,512]{2,1,0:T(4,128)(2,1)} fusion(bf16[4096,3,512]{2,1,0:T(4,128)(2,1)} %copy.19, s32[2048]{0:T(1024)S(1)} %fusion.7), kind=kCustom, calls=%fused_computation.1.clone | custom fusion | bytes 12591104 | tf_op jit(solution)/shard_map/jit(_take)/gather | solution.py:10
  432.1 27.0 %gather_fusion.2 = bf16[2048,3,512]{2,1,0:T(4,128)(2,1)} fusion(bf16[4096,3,512]{2,1,0:T(4,128)(2,1)} %copy.19, s32[2048]{0:T(1024)S(1)} %fusion.8), kind=kCustom, calls=%fused_computation.2.clone | custom fusion | bytes 12591104 | tf_op jit(solution)/shard_map/jit(_take)/gather | solution.py:10
  459.1 26.8 %gather_fusion.3 = bf16[2048,3,512]{2,1,0:T(4,128)(2,1)} fusion(bf16[4096,3,512]{2,1,0:T(4,128)(2,1)} %copy.19, s32[2048]{0:T(1024)S(1)} %fusion.9), kind=kCustom, calls=%fused_computation.3.clone | custom fusion | bytes 12591104 | tf_op jit(solution)/shard_map/jit(_take)/gather | solution.py:10
  485.9 103.7 %multiply_reduce_fusion.8 = (f32[2048,512]{1,0:T(8,128)}, f32[2048,512]{1,0:T(8,128)}, f32[2048,512]{1,0:T(8,128)}, f32[2048,512]{1,0:T(8,128)}, f32[2048,512]{1...) fusion(bf16[2048,3,512]{2,1,0:T(4,128)(2,1)} %gather_fusion, pred[2048]{0:T(1024)(128)(4,1)S(1)} %get-tuple-element.48, ...), kind=kLoop, calls=%fused_computation.13 | loop fusion | flops 68157440 | bytes 54552576 | tf_op jit(solution)/shard_map/reduce_sum | solution.py:31
  589.6 14.0 %fusion.5 = (f32[2048,1,512]{2,0,1:T(8,128)S(1)}, f32[2048,1,512]{2,0,1:T(8,128)S(1)}, f32[2048,1,512]{2,0,1:T(8,128)}, f32[2048,1,512]{2,0,1:T(8,128)}) fusion(f32[2048,512]{1,0:T(8,128)} %get-tuple-element.14, f32[2048,512]{1,0:T(8,128)} %get-tuple-element.15, f32[2048,512]{1,0:T(8,128)} %get-tuple-element.9, f32[512]{0:T(512)S(1)} %get-tuple-element.34, ...), kind=kLoop, calls=%fused_computation.32 | loop fusion | flops 13631488 | bytes 46143488 | tf_op jit(solution)/shard_map/mul | solution.py:35
  603.6 0.0 copy-start
  603.6 0.0 copy-start.1
  603.6 2.0 copy-done
  605.5 1.2 copy-done.1
  606.8 4.6 multiply_reduce_fusion.1
  611.4 98.9 %psum.7 = f32[2048]{0:T(1024)S(1)} all-reduce(f32[2048]{0:T(1024)S(1)} %multiply_reduce_fusion.1), channel_id=1, replica_groups=mesh['grp'=2,'cell'=16] {'cell'}, use_global_device_ids=true, to_apply=%region_8.10 | all-reduce | flops 2048 | bytes 16384 | tf_op jit(solution)/shard_map/psum | solution.py:50
  710.3 7.5 %multiply_reduce_fusion = (f32[512]{0:T(512)}, bf16[2048,4,512]{2,0,1:T(8,128)(2,1)S(1)}) fusion(f32[2048]{0:T(1024)S(1)} %add_rsqrt_fusion, f32[2048,1,512]{2,0,1:T(8,128)} %get-tuple-element.22, f32[2048,1,512]{2,0,1:T(8,128)} %get-tuple-element.23, f32[2048,1,512]{2,0,1:T(8,128)} %copy-done.1, f32[2048,1,512]{2,0,1:T(8,128)} %copy-done), kind=kLoop, calls=%fused_computation.5 | loop fusion | flops 29359616 | bytes 25176064 | tf_op jit(solution)/shard_map/reduce_sum | solution.py:53
  717.8 27.3 %copy.23 = bf16[2048,4,512]{2,1,0:T(4,128)(2,1)} copy(bf16[2048,4,512]{2,0,1:T(8,128)(2,1)S(1)} %get-tuple-element.17) | data formatting | bytes 16777216
  (12 shorter events, 0.2 us)
Async XLA Ops:
  25.6 7.7 %copy-start.5 = (f32[512]{0:T(512)S(1)}, f32[512]{0:T(512)}, u32[]{:S(2)}) copy-start(f32[512]{0:T(512)} %param.11) | copy-start | bytes 6148
  25.6 7.7 %copy-start.6 = (f32[512]{0:T(512)S(1)}, f32[512]{0:T(512)}, u32[]{:S(2)}) copy-start(f32[512]{0:T(512)} %param.12) | copy-start | bytes 6148
  25.6 7.8 %copy-start.3 = (f32[512]{0:T(512)S(1)}, f32[512]{0:T(512)}, u32[]{:S(2)}) copy-start(f32[512]{0:T(512)} %param.9) | copy-start | bytes 6148
  25.6 7.8 %copy-start.4 = (f32[512]{0:T(512)S(1)}, f32[512]{0:T(512)}, u32[]{:S(2)}) copy-start(f32[512]{0:T(512)} %param.10) | copy-start | bytes 6148
  25.6 7.8 %copy-start.2 = (s32[2048,4]{0,1:T(4,128)S(1)}, s32[2048,4]{0,1:T(4,128)}, u32[]{:S(2)}) copy-start(s32[2048,4]{0,1:T(4,128)} %param.13) | copy-start | bytes 98308
  25.6 304.4 %all-to-all-start = ((bf16[256,3,8192]{0,1,2:T(4,128)(2,1)}), bf16[256,3,8192]{0,1,2:T(4,128)(2,1)}, u32[]{:S(2)}, u32[]{:S(2)}) async-start(bf16[256,3,8192]{0,1,2:T(4,128)(2,1)} %copy.16), calls=%async_computation | async-start | bytes 33554432 | tf_op jit(solution)/shard_map/all_to_all | solution.py:47
  603.6 2.0 copy-start
  603.6 3.2 copy-start.1
where the time goes:
time: 747 us; the launch traced here: 745 us
  waiting for transfers between devices  296 us (40%)
  local copies, waits for them, and re-layouts  212 us (28%)
  other arithmetic  130 us (17%)
  blocking collectives  98.9 us (13%)
  starting transfers between devices  7.58 us (1%)
    all_to_all x1, waiting for transfers between devices, local(): lax.all_to_all(fields, 'cell', split_axis=2, concat_axis=0, tiled=True)  296 us
    gather x4, local copies, waits for them, and re-layouts, pick(): return jnp.take(grads, rows[:, column], axis=0).astype(jnp.float32)  107 us
    reduce_sum x1, other arithmetic, sensitivity(): inner = jnp.sum(source * receiver, axis=1)  104 us
    psum x1, blocking collectives, local(): total_sq = lax.psum(partial_sq, 'cell')  98.9 us
    unnamed x16, local copies, waits for them, and re-layouts  55.5 us
    all_to_all x3, local copies, waits for them, and re-layouts, local(): lax.all_to_all(fields, 'cell', split_axis=2, concat_axis=0, tiled=True)  48.6 us
  transfers between devices with their start and end apart: 1, of which 1 were waited for; matrix products, arithmetic and copies ran while one was open for 0% of the time, Pallas kernels for 0%

commit v1 on v0

--- a/solution.py
+++ b/solution.py
@@ -44,7 +44,10 @@
 def local(fields, horiz, vertical, tilt_angle, azimuth, electrode_quads):
     shards = lax.axis_size("cell")
     cell_dev = horiz.shape[0]
-    local_fields = lax.all_to_all(fields, "cell", split_axis=2, concat_axis=0, tiled=True)
+    local_fields = jnp.concatenate(
+        lax.all_to_all(jnp.stack(jnp.split(fields, lax.axis_size("cell"), axis=2)), "cell", 0, 0),
+        axis=0,
+    )
     values = sensitivity(local_fields, horiz, vertical, tilt_angle, azimuth, electrode_quads)
     partial_sq = jnp.sum(values * values, axis=(1, 2))
     total_sq = lax.psum(partial_sq, "cell")

time: 747 us -> 676 us (0.905)
  waiting for transfers between devices: 296 us -> 223 us
  local copies, waits for them, and re-layouts: 212 us -> 231 us
  blocking collectives: 98.9 us -> 81.9 us
    all_to_all x1, waiting for transfers between devices: 296 us -> 223 us  [local(): lax.all_to_all(jnp.stack(jnp.split(fields, lax.axis_size('cell'), axis=2)...]
    reshape x0 -> x1, local copies, waits for them, and re-layouts: none -> 53.9 us  [local(): jnp.concatenate(lax.all_to_all(jnp.stack(jnp.split(fields, lax.axis_size(...]
    all_to_all x3 -> x1, local copies, waits for them, and re-layouts: 48.6 us -> 6.26 us  [local(): lax.all_to_all(jnp.stack(jnp.split(fields, lax.axis_size('cell'), axis=2)...]
    psum x1, blocking collectives: 98.9 us -> 81.9 us  [local(): total_sq = lax.psum(partial_sq, 'cell')]
    unnamed x16 -> x30, local copies, waits for them, and re-layouts: 55.5 us -> 61.7 us
where the time goes in v1:
time: 676 us; the launch traced here: 675 us
  local copies, waits for them, and re-layouts  231 us (34%)
  waiting for transfers between devices  223 us (33%)
  other arithmetic  130 us (19%)
  blocking collectives  81.9 us (12%)
  starting transfers between devices  7.57 us (1%)
    all_to_all x1, waiting for transfers between devices, local(): lax.all_to_all(jnp.stack(jnp.split(fields, lax.axis_size('cell'), axis=2)...  223 us
    gather x4, local copies, waits for them, and re-layouts, pick(): return jnp.take(grads, rows[:, column], axis=0).astype(jnp.float32)  107 us
    reduce_sum x1, other arithmetic, sensitivity(): inner = jnp.sum(source * receiver, axis=1)  104 us
    psum x1, blocking collectives, local(): total_sq = lax.psum(partial_sq, 'cell')  81.9 us
    unnamed x30, local copies, waits for them, and re-layouts  61.7 us
    reshape x1, local copies, waits for them, and re-layouts, local(): jnp.concatenate(lax.all_to_all(jnp.stack(jnp.split(fields, lax.axis_size(...  53.9 us
    mul x1, other arithmetic, sensitivity(): -horiz * (inner - s_axis * r_axis)  14 us
  transfers between devices with their start and end apart: 1, of which 1 were waited for; matrix products, arithmetic and copies ran while one was open for 0% of the time, Pallas kernels for 0%

profile of v1, /device:TPU:0, one launch (start us, length us, event | category | flops | bytes accessed | tf_op | source)
XLA Modules:
  0.0 675.0 jit_solution(7523459773925047555)
XLA Ops:
  0.6 2.1 bitcast_dynamic-update-slice_fusion.15
  2.7 2.1 bitcast_dynamic-update-slice_fusion.14
  4.8 2.1 bitcast_dynamic-update-slice_fusion.13
  6.9 2.1 bitcast_dynamic-update-slice_fusion.12
  8.9 2.1 bitcast_dynamic-update-slice_fusion.11
  11.0 2.1 bitcast_dynamic-update-slice_fusion.10
  13.1 2.1 bitcast_dynamic-update-slice_fusion.9
  15.2 2.1 bitcast_dynamic-update-slice_fusion.8
  17.3 2.1 bitcast_dynamic-update-slice_fusion.7
  19.4 2.1 bitcast_dynamic-update-slice_fusion.6
  21.5 2.1 bitcast_dynamic-update-slice_fusion.5
  23.5 2.1 bitcast_dynamic-update-slice_fusion.4
  25.6 2.1 bitcast_dynamic-update-slice_fusion.3
  27.7 2.1 bitcast_dynamic-update-slice_fusion.2
  29.8 2.1 bitcast_dynamic-update-slice_fusion.1
  31.9 2.1 bitcast_dynamic-update-slice_fusion
  33.9 0.0 copy-start.5
  33.9 0.0 copy-start.6
  34.0 0.0 copy-start.3
  34.0 0.0 copy-start.4
  34.0 0.0 copy-start.2
  34.0 7.6 %all-to-all-start = ((bf16[16,256,3,512]{3,1,2,0:T(8,128)(2,1)}), bf16[16,256,3,512]{3,1,2,0:T(8,128)(2,1)}, u32[]{:S(2)}, u32[]{:S(2)}) async-start(bf16[16,256,3,512]{3,1,2,0:T(8,128)(2,1)} %bitcast_dynamic-update-slice_fusion), calls=%async_computation | async-start | bytes 25165824 | tf_op jit(solution)/shard_map/all_to_all | solution.py:48
  41.6 0.1 pad.6.clone
  41.6 0.0 copy-done.5
  41.6 0.0 copy-done.6
  41.7 0.0 copy-done.3
  41.7 0.0 copy-done.4
  41.8 0.1 pad_maximum_fusion.1
  41.8 0.0 copy-done.2
  41.9 223.4 %all-to-all-done = bf16[16,256,3,512]{3,1,2,0:T(8,128)(2,1)} async-done(((bf16[16,256,3,512]{3,1,2,0:T(8,128)(2,1)}), bf16[16,256,3,512]{3,1,2,0:T(8,128)(2,1)}, u32[]{:S(2)}, u32[]{:S(2)}) %all-to-all-start) | async-done | bytes 12582944 | tf_op jit(solution)/shard_map/all_to_all | solution.py:48
  265.3 6.3 copy.14
  271.6 53.9 %copy.15 = bf16[4096,3,512]{2,1,0:T(4,128)(2,1)} copy(bf16[4096,3,512]{2,0,1:T(8,128)(2,1)S(1)} %bitcast.83) | data formatting | bytes 25165824 | tf_op jit(solution)/shard_map/reshape | solution.py:47
  325.5 26.9 %gather_fusion.1 = bf16[2048,3,512]{2,1,0:T(4,128)(2,1)} fusion(bf16[4096,3,512]{2,1,0:T(4,128)(2,1)} %copy.15, s32[2048]{0:T(1024)S(1)} %get-tuple-element.44), kind=kCustom, calls=%fused_computation.1.clone | custom fusion | bytes 12591104 | tf_op jit(solution)/shard_map/jit(_take)/gather | solution.py:10
  352.4 27.0 %gather_fusion.2 = bf16[2048,3,512]{2,1,0:T(4,128)(2,1)} fusion(bf16[4096,3,512]{2,1,0:T(4,128)(2,1)} %copy.15, s32[2048]{0:T(1024)S(1)} %get-tuple-element.45), kind=kCustom, calls=%fused_computation.2.clone | custom fusion | bytes 12591104 | tf_op jit(solution)/shard_map/jit(_take)/gather | solution.py:10
  379.4 26.8 %gather_fusion.3 = bf16[2048,3,512]{2,1,0:T(4,128)(2,1)} fusion(bf16[4096,3,512]{2,1,0:T(4,128)(2,1)} %copy.15, s32[2048]{0:T(1024)S(1)} %get-tuple-element.46), kind=kCustom, calls=%fused_computation.3.clone | custom fusion | bytes 12591104 | tf_op jit(solution)/shard_map/jit(_take)/gather | solution.py:10
  406.2 26.7 %gather_fusion = bf16[2048,3,512]{2,1,0:T(4,128)(2,1)} fusion(bf16[4096,3,512]{2,1,0:T(4,128)(2,1)} %copy.15, s32[2048]{0:T(1024)S(1)} %get-tuple-element.43), kind=kCustom, calls=%fused_computation.clone | custom fusion | bytes 12591104 | tf_op jit(solution)/shard_map/jit(_take)/gather | solution.py:10
  432.8 103.7 %multiply_reduce_fusion.8 = (f32[2048,512]{1,0:T(8,128)}, f32[2048,512]{1,0:T(8,128)}, f32[2048,512]{1,0:T(8,128)}, f32[2048,512]{1,0:T(8,128)}, f32[2048,512]{1...) fusion(bf16[2048,3,512]{2,1,0:T(4,128)(2,1)} %gather_fusion, pred[2048]{0:T(1024)(128)(4,1)S(1)} %get-tuple-element.52, ...), kind=kLoop, calls=%fused_computation.13 | loop fusion | flops 68157440 | bytes 54552576 | tf_op jit(solution)/shard_map/reduce_sum | solution.py:31
  536.5 14.0 %fusion.5 = (f32[2048,1,512]{2,0,1:T(8,128)S(1)}, f32[2048,1,512]{2,0,1:T(8,128)S(1)}, f32[2048,1,512]{2,0,1:T(8,128)}, f32[2048,1,512]{2,0,1:T(8,128)}) fusion(f32[2048,512]{1,0:T(8,128)} %get-tuple-element.14, f32[2048,512]{1,0:T(8,128)} %get-tuple-element.15, f32[2048,512]{1,0:T(8,128)} %get-tuple-element.9, f32[512]{0:T(512)S(1)} %get-tuple-element.34, ...), kind=kLoop, calls=%fused_computation.32 | loop fusion | flops 13631488 | bytes 46143488 | tf_op jit(solution)/shard_map/mul | solution.py:35
  550.5 0.0 copy-start
  550.5 0.0 copy-start.1
  550.5 2.0 copy-done
  552.5 1.2 copy-done.1
  553.7 4.6 multiply_reduce_fusion.1
  558.3 81.9 %psum.7 = f32[2048]{0:T(1024)S(1)} all-reduce(f32[2048]{0:T(1024)S(1)} %multiply_reduce_fusion.1), channel_id=1, replica_groups=mesh['grp'=2,'cell'=16] {'cell'}, use_global_device_ids=true, to_apply=%region_8.10 | all-reduce | flops 2048 | bytes 16384 | tf_op jit(solution)/shard_map/psum | solution.py:53
  640.2 7.5 %multiply_reduce_fusion = (f32[512]{0:T(512)}, bf16[2048,4,512]{2,0,1:T(8,128)(2,1)S(1)}) fusion(f32[2048]{0:T(1024)S(1)} %add_rsqrt_fusion, f32[2048,1,512]{2,0,1:T(8,128)} %get-tuple-element.22, f32[2048,1,512]{2,0,1:T(8,128)} %get-tuple-element.23, f32[2048,1,512]{2,0,1:T(8,128)} %copy-done.1, f32[2048,1,512]{2,0,1:T(8,128)} %copy-done), kind=kLoop, calls=%fused_computation.5 | loop fusion | flops 29359616 | bytes 25176064 | tf_op jit(solution)/shard_map/reduce_sum | solution.py:56
  647.7 27.3 %copy.19 = bf16[2048,4,512]{2,1,0:T(4,128)(2,1)} copy(bf16[2048,4,512]{2,0,1:T(8,128)(2,1)S(1)} %get-tuple-element.17) | data formatting | bytes 16777216
  (10 shorter events, 0.1 us)
Async XLA Ops:
  33.9 7.7 %copy-start.5 = (f32[512]{0:T(512)S(1)}, f32[512]{0:T(512)}, u32[]{:S(2)}) copy-start(f32[512]{0:T(512)} %param.11) | copy-start | bytes 6148
  33.9 7.7 %copy-start.6 = (f32[512]{0:T(512)S(1)}, f32[512]{0:T(512)}, u32[]{:S(2)}) copy-start(f32[512]{0:T(512)} %param.12) | copy-start | bytes 6148
  34.0 7.8 %copy-start.3 = (f32[512]{0:T(512)S(1)}, f32[512]{0:T(512)}, u32[]{:S(2)}) copy-start(f32[512]{0:T(512)} %param.9) | copy-start | bytes 6148
  34.0 7.8 %copy-start.4 = (f32[512]{0:T(512)S(1)}, f32[512]{0:T(512)}, u32[]{:S(2)}) copy-start(f32[512]{0:T(512)} %param.10) | copy-start | bytes 6148
  34.0 7.9 %copy-start.2 = (s32[2048,4]{0,1:T(4,128)S(1)}, s32[2048,4]{0,1:T(4,128)}, u32[]{:S(2)}) copy-start(s32[2048,4]{0,1:T(4,128)} %param.13) | copy-start | bytes 98308
  34.0 231.3 %all-to-all-start = ((bf16[16,256,3,512]{3,1,2,0:T(8,128)(2,1)}), bf16[16,256,3,512]{3,1,2,0:T(8,128)(2,1)}, u32[]{:S(2)}, u32[]{:S(2)}) async-start(bf16[16,256,3,512]{3,1,2,0:T(8,128)(2,1)} %bitcast_dynamic-update-slice_fusion), calls=%async_computation | async-start | bytes 25165824 | tf_op jit(solution)/shard_map/all_to_all | solution.py:48
  550.5 2.0 copy-start
  550.5 3.2 copy-start.1
